TPU v7x, 512 devices: a whole 4x8x8 slice. The times are simulated.
512 devices in a mesh: cell: 8 (over z), donor: 8 (over x, core), gene: 8 (over y).
Axes of the slice: x: 4, y: 8, z: 8, core: 2. Of those that a mesh axis runs over, the one named last changes fastest.
Arguments:
- counts: int32 [32768, 2048], P(('cell', 'donor'), 'gene'), may hold values from 0 to 35
- cell_donor: int32 [32768], P(('cell', 'donor')), may hold values from 0 to 511, as said below
- cell_type: int32 [32768], P(('cell', 'donor')), may hold values from -1 to 23, as said below
- covariates: float32 [512, 50], P(('cell', 'donor')), may hold values from -6 to 6
- dosage: int32 [8192, 512], P('gene'), may hold values from 0 to 2
- windows: int32 [2048, 1024], P(('gene', 'cell', 'donor')), may hold values from -1 to 8191, as said below
Outputs:
- association: float32 [24, 2048, 1024], P(None, ('gene', 'cell', 'donor'))
Inputs may be any that keep to these rules, and one draw needn't show every extreme that they name: `cell_donor`: rows come in blocks of 512: a row of block b names a donor d with (d // 8) % 8 = b % 8. Every donor has at least one cell of every cell type. `cell_type`: in each block of 512 rows the live slots (type 0 or more) come first and the empty ones (-1) last; the number of live slots varies from block to block and some block is full. `windows`: row j lists consecutive SNP numbers in ascending order, then -1 to its end; all of them lie in [b * 1024, (b + 1) * 1024) with b = j // 256. A window holds 512 to 1024 SNPs, some window holds exactly 1024, and the last gene's window ends at the last SNP.
All inputs are finite; a program needn't handle non-finite values.
Results may differ from a plain program's by a relative error of at most 0.00045.
Values sent between devices are 32-bit elements; how exact they have to be, the bound alone decides.
No kernel may reach another device: no remote copies, remote signals or barrier semaphores. Data moves between devices by JAX's collectives and lax.ppermute only.
A program may use at most 64 MiB of HBM per device.

v0:
```python
import math
import jax
import jax.numpy as jnp
from jax import lax
from jax.sharding import PartitionSpec as P

CT = 24


def log_cpm(pseudobulk, library):
    return jnp.log2((pseudobulk + 0.5) / (library + 1.0) * 1000000.0)


def with_intercept(covariates):
    intercept = jnp.ones((covariates.shape[0], 1), jnp.float32)
    return jnp.concatenate([intercept, covariates], axis=1)


def factor_lower(gram_sum):
    order = gram_sum.shape[0]
    factor = jnp.zeros_like(gram_sum)
    for column in range(order):
        known = factor[column, :column]
        pivot = jnp.sqrt(gram_sum[column, column] - jnp.sum(known * known))
        factor = factor.at[column, column].set(pivot)
        if column + 1 < order:
            below = gram_sum[column + 1 :, column] - jnp.dot(
                factor[column + 1 :, :column], known, precision=lax.Precision.HIGHEST
            )
            factor = factor.at[column + 1 :, column].set(below / pivot)
    return factor


def solve_written(factor, right_rows):
    order = factor.shape[0]
    forward = []
    for row in range(order):
        value = right_rows[row]
        if row > 0:
            value = value - jnp.dot(
                factor[row, :row], jnp.stack(forward), precision=lax.Precision.HIGHEST
            )
        forward.append(value / factor[row, row])
    backward = [None] * order
    for row in range(order - 1, -1, -1):
        value = forward[row]
        if row < order - 1:
            later = jnp.stack(backward[row + 1 :])
            value = value - jnp.dot(factor[row + 1 :, row], later, precision=lax.Precision.HIGHEST)
        backward[row] = value / factor[row, row]
    return jnp.stack(backward)


def solve_normal(gram_sum, cross_sum):
    order = gram_sum.shape[0]
    factor = factor_lower(gram_sum)
    inverse = solve_written(factor, jnp.eye(order, dtype=jnp.float32))
    return jnp.einsum("kj,cjg->ckg", inverse, cross_sum, precision=lax.Precision.HIGHEST)


def association_block(residual, dosage, windows, first_snp):
    window_len = windows.shape[1]
    every_snp = jnp.einsum(
        "sd,dcg->gsc", dosage.astype(jnp.float32), residual, precision=lax.Precision.HIGHEST
    )
    padded = jnp.pad(every_snp, ((0, 0), (0, window_len), (0, 0)))
    starts = windows[:, 0] - first_snp
    gene_ids = jnp.arange(windows.shape[0], dtype=jnp.int32)

    def one_gene(pair):
        gene_id, start = pair
        gene_rows = lax.dynamic_index_in_dim(padded, gene_id, 0, keepdims=False)
        return lax.dynamic_slice_in_dim(gene_rows, start, window_len, 0)

    sliced = lax.map(one_gene, (gene_ids, starts))
    products = jnp.transpose(sliced, (2, 0, 1))
    scaling = 1.0 / math.sqrt(dosage.shape[1])
    return jnp.where((windows >= 0)[None], products, 0.0) * scaling


def owner_index(cell_donor, cell_type, donors_here, groups):
    cell_slot = cell_donor // (donors_here * groups)
    local_donor = cell_slot * donors_here + cell_donor % donors_here
    return jnp.where(cell_type >= 0, local_donor * CT + cell_type, -1)


def per_device(counts, cell_donor, cell_type, covariates, dosage, windows):
    groups = lax.axis_size("donor")
    donors_here = covariates.shape[0]
    cell_count = counts.shape[0]
    owner_slot = owner_index(cell_donor, cell_type, donors_here, groups)
    counts_half = counts.astype(jnp.bfloat16)
    first_snp = lax.axis_index("gene") * dosage.shape[0]
    row_ids = lax.broadcasted_iota(
        jnp.int32, (donors_here * CT * lax.axis_size("cell"), cell_count), 0
    )
    onehot_table = (row_ids == owner_slot[None, :]).astype(jnp.bfloat16)
    pseudobulk = lax.psum_scatter(
        jnp.dot(onehot_table, counts_half, preferred_element_type=jnp.float32),
        "cell",
        scatter_dimension=0,
        tiled=True,
    )
    library = lax.psum(jnp.sum(pseudobulk, axis=1), "gene")
    expression = log_cpm(pseudobulk, library[:, None]).reshape(donors_here, CT, -1)
    design = with_intercept(covariates)
    gram_part = jnp.dot(design.T, design, precision=lax.Precision.HIGHEST)
    cross_part = jnp.einsum("dk,dcg->ckg", design, expression, precision=lax.Precision.HIGHEST)
    gram_sum, cross_sum = lax.psum((gram_part, cross_part), ("cell", "donor"))
    coefficients = solve_normal(gram_sum, cross_sum)
    residual = expression - jnp.einsum(
        "dk,ckg->dcg", design, coefficients, precision=lax.Precision.HIGHEST
    )
    regrouped = lax.all_to_all(residual, ("cell", "donor"), split_axis=2, concat_axis=0, tiled=True)
    return association_block(regrouped, dosage, windows, first_snp)


def solution(mesh):
    in_specs = (
        P(("cell", "donor"), "gene"),
        P(("cell", "donor")),
        P(("cell", "donor")),
        P(("cell", "donor"), None),
        P("gene", None),
        P(("gene", "cell", "donor"), None),
    )
    out_specs = P(None, ("gene", "cell", "donor"), None)
    return jax.shard_map(
        per_device, mesh=mesh, in_specs=in_specs, out_specs=out_specs, check_vma=False
    )
```

profile of v0, /device:TPU:1, one launch (start us, length us, event | category | flops | bytes accessed | tf_op | source)
XLA Modules:
  0.0 813.1 jit_solution(3078640551746485459)
XLA Ops:
  7.3 2.8 fusion
  10.5 252.7 %psum.23 = f32[51,51]{1,0:T(8,128)S(1)} all-reduce(f32[51,51]{1,0:T(8,128)S(1)} %fusion.449), channel_id=1, replica_groups=mesh['cell'=8,'donor'=8,'gene'=8] {'cell','donor'}, use_global_device_ids=true, to_apply=%region_4.5 | all-reduce | flops 2601 | bytes 20808 | tf_op jit(solution)/shard_map/psum | solution.py:109
  375.8 11.7 %scatter.456 = f32[51,51]{1,0:T(8,128)S(1)} dynamic-update-slice(f32[51,51]{1,0:T(8,128)S(1)} %copy.362, f32[1,1]{1,0:T(1,128)} %bitcast.220, s32[]{:T(128)} %constant.2846.clone.1, s32[]{:T(128)} %constant.2846.clone.1) | dynamic-update-slice | bytes 12 | tf_op jit(solution)/shard_map/scatter | solution.py:25
  431.1 1.8 fusion.481
  497.7 0.8 fusion.295
  510.8 0.8 fusion.321
  517.2 1.0 reduce_sum.454
  518.2 14.1 %psum.21 = f32[192]{0:T(256)S(1)} all-reduce(f32[192]{0:T(256)S(1)} %reduce_sum.454), channel_id=1, replica_groups=mesh['cell'=8,'donor'=8,'gene'=8] {'gene'}, use_global_device_ids=true, to_apply=%region_2.3 | all-reduce | flops 192 | bytes 1536 | tf_op jit(solution)/shard_map/psum | solution.py:104
  532.3 1.0 log_multiply_fusion
  533.3 2.5 convolution_bitcast_fusion.1
  537.1 1.4 fusion.335
  539.7 193.4 %all-reduce.5.cloned.1.call-done = f32[24,51,256]{2,1,0:T(8,128)} async-done(((f32[24,51,256]{2,1,0:T(8,128)}), f32[24,51,256]{2,1,0:T(8,128)}) %all-reduce.5.cloned.1.call-update) | async-done | bytes 1253392 | tf_op jit(solution)/shard_map/psum | solution.py:109
  733.0 2.6 convolution_bitcast_fusion
  736.9 1.5 reshape.3475
  738.4 9.8 %all-to-all-start = ((f32[64,1,768]{2,1,0:T(1,128)}), f32[64,1,768]{2,1,0:T(1,128)S(1)}, u32[]{:S(2)}, u32[]{:S(2)}) async-start(f32[64,1,768]{2,1,0:T(1,128)} %reshape.3475), calls=%async_computation.1 | async-start | bytes 393216 | tf_op jit(solution)/shard_map/all_to_all | solution.py:114
  748.3 11.7 %all-to-all-done = f32[64,1,768]{2,1,0:T(1,128)S(1)} async-done(((f32[64,1,768]{2,1,0:T(1,128)}), f32[64,1,768]{2,1,0:T(1,128)S(1)}, u32[]{:S(2)}, u32[]{:S(2)}) %all-to-all-start) | async-done | bytes 196640 | tf_op jit(solution)/shard_map/all_to_all | solution.py:114
  760.6 1.2 reduce.398
  762.6 6.8 fusion.5
  769.4 34.5 %while.115 = (s32[]{:T(128)}, f32[4,1024,24]{1,0,2:T(4,128)}, s32[4]{0:T(128)S(1)}, s32[4]{0:T(128)S(1)}, f32[4,2048,24]{1,2,0:T(8,128)S(1)}) while((s32[]{:T(128)}, f32[4,1024,24]{1,0,2:T(4,128)}, s32[4]{0:T(128)S(1)}, s32[4]{0:T(128)S(1)}, f32[4,2048,24]{1,2,0:T(8,128)S(1)}) %tuple.543), condition=%wide.region_55.56_spmd.clone, body=%wide.region_54.55_spmd.sunk.clone | while | flops 10 | bytes 590021 | solution.py:75
  775.1 2.9 dynamic_update_slice.10
  783.8 2.9 dynamic_update_slice.10
  792.4 2.9 dynamic_update_slice.10
  801.0 2.9 dynamic_update_slice.10
  803.9 1.9 multiply_bitcast_fusion
  (625 shorter events, 181.2 us)
Async XLA Ops:
  6.5 510.6 %reduce-scatter.2.cloned.1.call-start = ((), (), s32[]{:S(2)}) async-start(), calls=%async_computation.2 | async-start | bytes 1769472 | tf_op jit(solution)/shard_map/reduce_scatter | solution.py:98
  7.2 2.9 copy-start.1
  10.1 722.9 %all-reduce.5.cloned.1.call-start = ((), (), s32[]{:S(2)}) async-start(), calls=%async_computation.3 | async-start | bytes 2752512 | tf_op jit(solution)/shard_map/psum | solution.py:109
  736.4 11.7 %copy-start.2 = (s32[4,1024]{1,0:T(4,128)S(1)}, s32[4,1024]{1,0:T(4,128)}, u32[]{:S(2)}) copy-start(s32[4,1024]{1,0:T(4,128)} %param.215) | copy-start | bytes 49156
  736.9 25.7 %copy-start = (s32[1024,512]{1,0:T(8,128)S(1)}, s32[1024,512]{1,0:T(8,128)}, u32[]{:S(2)}) copy-start(s32[1024,512]{1,0:T(8,128)} %param.214) | copy-start | bytes 6291460
  738.4 21.7 %all-to-all-start = ((f32[64,1,768]{2,1,0:T(1,128)}), f32[64,1,768]{2,1,0:T(1,128)S(1)}, u32[]{:S(2)}, u32[]{:S(2)}) async-start(f32[64,1,768]{2,1,0:T(1,128)} %reshape.3475), calls=%async_computation.1 | async-start | bytes 393216 | tf_op jit(solution)/shard_map/all_to_all | solution.py:114
Sparse Core Ops, SparseCore 0:
  10.3 45.2 reduce-scatter.1
  535.9 197.0 all-reduce.4
where the time goes:
time: 824 us; the launch traced here: 813 us
  blocking collectives  267 us (32%)
  waiting for transfers between devices  205 us (25%)
  matrix products  96.3 us (12%)
  local copies, waits for them, and re-layouts  94.6 us (11%)
  between operations  84 us (10%)
  other arithmetic  39.8 us (5%)
  loops' own time  16.7 us (2%)
  starting transfers between devices  9.82 us (1%)
    psum x1, blocking collectives, per_device(): gram_sum, cross_sum = lax.psum((gram_part, cross_part), ('cell', 'donor'))  253 us
    psum x1, waiting for transfers between devices, per_device(): gram_sum, cross_sum = lax.psum((gram_part, cross_part), ('cell', 'donor'))  193 us
    dot_general x49, matrix products, solve_written(): jnp.dot(factor[row + 1:, row], later, precision=lax.Precision.HIGHEST)  37.7 us
    dot_general x49, matrix products, solve_written(): jnp.dot(factor[row, :row], jnp.stack(forward), precision=lax.Precision.HI...  36.4 us
    reduce_sum x49, other arithmetic, factor_lower(): pivot = jnp.sqrt(gram_sum[column, column] - jnp.sum(known * known))  30 us
    scatter x50, local copies, waits for them, and re-layouts, factor_lower(): factor = factor.at[column + 1:, column].set(below / pivot)  19.3 us
    scatter x50, local copies, waits for them, and re-layouts, factor_lower(): factor = factor.at[column, column].set(pivot)  18.7 us
    another operation x1, loops' own time, association_block(): sliced = lax.map(one_gene, (gene_ids, starts))  16.7 us
  transfers between devices with their start and end apart: 3, of which 2 were waited for; matrix products, arithmetic and copies ran while one was open for 23% of the time, Pallas kernels for 0%

commit v1 on v0

--- a/solution.py
+++ b/solution.py
@@ -106,7 +106,12 @@
     design = with_intercept(covariates)
     gram_part = jnp.dot(design.T, design, precision=lax.Precision.HIGHEST)
     cross_part = jnp.einsum("dk,dcg->ckg", design, expression, precision=lax.Precision.HIGHEST)
-    gram_sum, cross_sum = lax.psum((gram_part, cross_part), ("cell", "donor"))
+
+    def _lift_bands(incoming_x):
+        t_next = lax.psum(incoming_x, "donor")
+        return lax.psum(t_next, "cell")
+
+    gram_sum, cross_sum = _lift_bands((gram_part, cross_part))
     coefficients = solve_normal(gram_sum, cross_sum)
     residual = expression - jnp.einsum(
         "dk,ckg->dcg", design, coefficients, precision=lax.Precision.HIGHEST

time: 824 us -> 572 us (0.69)
  blocking collectives: 267 us -> 67.7 us
  waiting for transfers between devices: 205 us -> 161 us
  local copies, waits for them, and re-layouts: 94.6 us -> 85.6 us
    psum x1 -> x2, blocking collectives: 253 us -> 53.6 us  [the longest x1 27 us: _lift_bands(): t_next = lax.psum(incoming_x, 'donor')]
    psum x1 -> x2, waiting for transfers between devices: 193 us -> 149 us  [the longest x1 75.2 us: _lift_bands(): return lax.psum(t_next, 'cell')]
    dynamic_update_slice x8, local copies, waits for them, and re-layouts: 12.1 us -> 3.65 us  [association_block(): sliced = lax.map(one_gene, (gene_ids, starts))]
  transfers between devices with their start and end apart: 3 -> 4, of which waited for: 2 -> 3; matrix products, arithmetic and copies ran while one was open for 23% -> 33% of each run, Pallas kernels for 0% -> 0%
where the time goes in v1:
time: 572 us; the launch traced here: 561 us
  waiting for transfers between devices  161 us (28%)
  matrix products  95.7 us (17%)
  local copies, waits for them, and re-layouts  85.6 us (15%)
  between operations  83.7 us (15%)
  blocking collectives  67.7 us (12%)
  other arithmetic  38.9 us (7%)
  loops' own time  15.7 us (3%)
  starting transfers between devices  12.7 us (2%)
    psum x1, waiting for transfers between devices, _lift_bands(): return lax.psum(t_next, 'cell')  75.2 us
    psum x1, waiting for transfers between devices, _lift_bands(): t_next = lax.psum(incoming_x, 'donor')  74.2 us
    dot_general x49, matrix products, solve_written(): jnp.dot(factor[row + 1:, row], later, precision=lax.Precision.HIGHEST)  37.4 us
    dot_general x49, matrix products, solve_written(): jnp.dot(factor[row, :row], jnp.stack(forward), precision=lax.Precision.HI...  36.2 us
    reduce_sum x49, other arithmetic, factor_lower(): pivot = jnp.sqrt(gram_sum[column, column] - jnp.sum(known * known))  30 us
    psum x1, blocking collectives, _lift_bands(): t_next = lax.psum(incoming_x, 'donor')  27 us
    psum x1, blocking collectives, _lift_bands(): return lax.psum(t_next, 'cell')  26.6 us
    scatter x50, local copies, waits for them, and re-layouts, factor_lower(): factor = factor.at[column + 1:, column].set(below / pivot)  19.3 us
  transfers between devices with their start and end apart: 4, of which 3 were waited for; matrix products, arithmetic and copies ran while one was open for 33% of the time, Pallas kernels for 0%

profile of v1, /device:TPU:1, one launch (start us, length us, event | category | flops | bytes accessed | tf_op | source)
XLA Modules:
  0.0 561.2 jit_solution(1532693309045555996)
XLA Ops:
  7.3 2.8 fusion
  10.5 27.0 %psum.38 = f32[51,51]{1,0:T(8,128)S(1)} all-reduce(f32[51,51]{1,0:T(8,128)S(1)} %fusion.449), channel_id=1, replica_groups=mesh['cell'=8,'donor'=8,'gene'=8] {'donor'}, use_global_device_ids=true, to_apply=%region_5.6 | all-reduce | flops 2601 | bytes 20808 | tf_op jit(solution)/shard_map/psum | solution.py:111
  37.5 26.6 %psum.39 = f32[51,51]{1,0:T(8,128)S(1)} all-reduce(f32[51,51]{1,0:T(8,128)S(1)} %psum.38), channel_id=1, replica_groups=mesh['cell'=8,'donor'=8,'gene'=8] {'cell'}, use_global_device_ids=true, to_apply=%region_6.7 | all-reduce | flops 2601 | bytes 20808 | tf_op jit(solution)/shard_map/psum | solution.py:112
  176.8 11.7 %scatter.456 = f32[51,51]{1,0:T(8,128)S(1)} dynamic-update-slice(f32[51,51]{1,0:T(8,128)S(1)} %copy.363, f32[1,1]{1,0:T(1,128)} %bitcast.220, s32[]{:T(128)} %constant.2846.clone.1, s32[]{:T(128)} %constant.2846.clone.1) | dynamic-update-slice | bytes 12 | tf_op jit(solution)/shard_map/scatter | solution.py:25
  231.1 1.8 fusion.481
  270.5 0.8 fusion.250
  276.1 0.8 fusion.370
  296.7 0.8 fusion.293
  300.9 0.8 fusion.301
  311.4 1.0 reduce_sum.454
  312.5 14.1 %psum.35 = f32[192]{0:T(256)S(1)} all-reduce(f32[192]{0:T(256)S(1)} %reduce_sum.454), channel_id=1, replica_groups=mesh['cell'=8,'donor'=8,'gene'=8] {'gene'}, use_global_device_ids=true, to_apply=%region_2.3 | all-reduce | flops 192 | bytes 1536 | tf_op jit(solution)/shard_map/psum | solution.py:104
  326.5 1.0 log_multiply_fusion
  327.6 2.5 convolution_bitcast_fusion.1
  332.8 74.2 %all-reduce.6.cloned.1.call-done = f32[24,51,256]{2,1,0:T(8,128)} async-done(((f32[24,51,256]{2,1,0:T(8,128)}), f32[24,51,256]{2,1,0:T(8,128)}) %all-reduce.6.cloned.1.call-update) | async-done | bytes 1253392 | tf_op jit(solution)/shard_map/psum | solution.py:111
  412.2 1.4 fusion.335
  414.8 75.2 %all-reduce.8.cloned.1.call-done = f32[24,51,256]{2,1,0:T(8,128)} async-done(((f32[24,51,256]{2,1,0:T(8,128)}), f32[24,51,256]{2,1,0:T(8,128)}) %all-reduce.8.cloned.1.call-update) | async-done | bytes 1253392 | tf_op jit(solution)/shard_map/psum | solution.py:112
  490.0 2.6 convolution_bitcast_fusion
  493.8 1.5 reshape.3475
  495.3 12.4 %all-to-all-start = ((f32[64,1,768]{2,1,0:T(1,128)}), f32[64,1,768]{2,1,0:T(1,128)S(1)}, u32[]{:S(2)}, u32[]{:S(2)}) async-start(f32[64,1,768]{2,1,0:T(1,128)} %reshape.3475), calls=%async_computation.1 | async-start | bytes 393216 | tf_op jit(solution)/shard_map/all_to_all | solution.py:119
  507.9 11.7 %all-to-all-done = f32[64,1,768]{2,1,0:T(1,128)S(1)} async-done(((f32[64,1,768]{2,1,0:T(1,128)}), f32[64,1,768]{2,1,0:T(1,128)S(1)}, u32[]{:S(2)}, u32[]{:S(2)}) %all-to-all-start) | async-done | bytes 196640 | tf_op jit(solution)/shard_map/all_to_all | solution.py:119
  520.2 1.1 reduce.398
  522.2 6.6 %fusion.5 = f32[4,1024,24]{1,2,0:T(8,128)S(1)} fusion(s32[1024,512]{1,0:T(8,128)S(1)} %copy-done, f32[64,8,24,4]{2,1,3,0:T(8,128)S(1)} %bitcast.2482), kind=kOutput, calls=%fused_computation.9 | convolution fusion | flops 604504064 | bytes 2686976 | tf_op jit(solution)/shard_map/sd,dcg->gsc/dot_general | solution.py:63
  528.9 24.5 %while.115 = (s32[]{:T(128)}, f32[4,1024,24]{1,0,2:T(4,128)S(1)}, s32[4]{0:T(128)S(1)}, s32[4]{0:T(128)S(1)}, f32[4,2048,24]{1,2,0:T(8,128)S(1)}) while((s32[]{:T(128)}, f32[4,1024,24]{1,0,2:T(4,128)S(1)}, s32[4]{0:T(128)S(1)}, s32[4]{0:T(128)S(1)}, f32[4,2048,24]{1,2,0:T(8,128)S(1)}) %tuple.552), condition=%wide.region_57.58_spmd.clone, body=%wide.region_56.57_spmd.sunk.clone | while | flops 10 | bytes 590021 | solution.py:75
  553.4 0.9 multiply_bitcast_fusion
  (631 shorter events, 182.1 us)
Async XLA Ops:
  6.5 304.9 %reduce-scatter.2.cloned.1.call-start = ((), (), s32[]{:S(2)}) async-start(), calls=%async_computation.2 | async-start | bytes 1769472 | tf_op jit(solution)/shard_map/reduce_scatter | solution.py:98
  7.2 2.9 copy-start.2
  10.1 396.9 %all-reduce.6.cloned.1.call-start = ((), (), s32[]{:S(2)}) async-start(), calls=%async_computation.3 | async-start | bytes 2752512 | tf_op jit(solution)/shard_map/psum | solution.py:111
  330.1 159.9 %all-reduce.8.cloned.1.call-start = ((), (), s32[]{:S(2)}) async-start(), calls=%async_computation.4 | async-start | bytes 2752512 | tf_op jit(solution)/shard_map/psum | solution.py:112
  493.4 14.4 %copy-start.3 = (s32[4,1024]{1,0:T(4,128)S(1)}, s32[4,1024]{1,0:T(4,128)}, u32[]{:S(2)}) copy-start(s32[4,1024]{1,0:T(4,128)} %param.215) | copy-start | bytes 49156
  493.8 28.3 %copy-start = (s32[1024,512]{1,0:T(8,128)S(1)}, s32[1024,512]{1,0:T(8,128)}, u32[]{:S(2)}) copy-start(s32[1024,512]{1,0:T(8,128)} %param.214) | copy-start | bytes 6291460
  495.3 24.3 %all-to-all-start = ((f32[64,1,768]{2,1,0:T(1,128)}), f32[64,1,768]{2,1,0:T(1,128)S(1)}, u32[]{:S(2)}, u32[]{:S(2)}) async-start(f32[64,1,768]{2,1,0:T(1,128)} %reshape.3475), calls=%async_computation.1 | async-start | bytes 393216 | tf_op jit(solution)/shard_map/all_to_all | solution.py:119
  522.1 6.7 %copy-start.1 = (f32[4,1024,24]{1,0,2:T(4,128)S(1)}, f32[4,1024,24]{1,0,2:T(4,128)}, u32[]{:S(2)}) copy-start(f32[4,1024,24]{1,0,2:T(4,128)} %custom-call) | copy-start | bytes 1179652
Sparse Core Ops, SparseCore 0:
  10.3 45.5 reduce-scatter.1
  330.2 76.7 all-reduce.5
  409.5 80.4 all-reduce.7
